TPU v7x, 32 devices: a whole 2x2x4 slice. The times are simulated.
32 devices in a mesh: dp: 8 (over z, y), mp: 4 (over x, core).
Axes of the slice: x: 2, y: 2, z: 4, core: 2. Of those that a mesh axis runs over, the one named last changes fastest.
Arguments:
- student: bfloat16 [384, 16, 1280], P('dp'), may hold values from -6 to 6
- dino_target: bfloat16 [256, 16, 1536], P('dp', None, 'mp'), may hold values from -6 to 6
- siglip_target: bfloat16 [256, 16, 1152], P('dp', None, 'mp'), may hold values from -6 to 6
- clip_target: bfloat16 [256, 16, 1024], P('dp', None, 'mp'), may hold values from -6 to 6
- image_owner: int32 [256, 1], replicated, may hold values from 0 to 7; in each aligned block of 32 rows (0 to 31, 32 to 63, ...) at most 6 rows name the same one
- patch_count: int32 [256], replicated, may hold values from 1 to 16
- dino_expand: bfloat16 [1280, 1536], P(None, 'mp'), may hold values from -0.15625 to 0.15625
- dino_project: bfloat16 [1536, 1536], P('mp'), may hold values from -0.15625 to 0.15625
- siglip_expand: bfloat16 [1280, 1536], P(None, 'mp'), may hold values from -0.15625 to 0.15625
- siglip_project: bfloat16 [1536, 1152], P('mp'), may hold values from -0.15625 to 0.15625
- clip_expand: bfloat16 [1280, 1536], P(None, 'mp'), may hold values from -0.15625 to 0.15625
- clip_project: bfloat16 [1536, 1024], P('mp'), may hold values from -0.15625 to 0.15625
Outputs:
- student_grad: bfloat16 [384, 16, 1280], P('dp', None, 'mp')
- dino_expand_grad: float32 [1280, 1536], P('dp', 'mp')
- dino_project_grad: float32 [1536, 1536], P('mp', 'dp')
- siglip_expand_grad: float32 [1280, 1536], P('dp', 'mp')
- siglip_project_grad: float32 [1536, 1152], P('mp', 'dp')
- clip_expand_grad: float32 [1280, 1536], P('dp', 'mp')
- clip_project_grad: float32 [1536, 1024], P('mp', 'dp')
Inputs may be any that keep to these rules, and one draw needn't show every extreme that they name: `image_owner`: within each aligned block of 32 images (one store shard) no owner is named more than 6 times; every owner is named by some image.
All inputs are finite; a program needn't handle non-finite values.
Results may differ from a plain program's by a relative error of at most 0.028.
Values may be sent and summed in bfloat16 or wider, within the bound.
A program may use at most 128 MiB of HBM per device.

v0:
```python
import jax
import jax.numpy as jnp
from jax import lax
from jax.sharding import PartitionSpec as P


def for_sending(value):

    def short(part):
        return part.astype(jnp.bfloat16) if part.dtype == jnp.float32 else part

    return jax.tree.map(short, value)


def gelu_parts(hidden):
    normal_cdf = 0.5 * (1.0 + jax.scipy.special.erf(hidden * 0.7071067811865476))
    density = jnp.exp(-0.5 * hidden * hidden) * 0.3989422804014327
    return (hidden * normal_cdf, normal_cdf + hidden * density)


def selection(store_block, owner_ids, capacity):
    belongs = (owner_ids[:, None] == store_block[None, :]).astype(jnp.int32)
    position = jnp.cumsum(belongs, axis=1) - 1
    ranks = jnp.arange(capacity, dtype=jnp.int32)
    return belongs[:, None, :] * (position[:, None, :] == ranks[None, :, None]).astype(jnp.int32)


def fold_step(activated, project, segment):
    back_sum = lax.dot_general(
        segment, project, (((1,), (1,)), ((), ())), preferred_element_type=jnp.float32
    )
    update = lax.dot_general(
        activated, segment, (((0,), (0,)), ((), ())), preferred_element_type=jnp.float32
    )
    return (back_sum, update)


def first_term(inputs, hidden_grad, loss_scale):
    return (
        lax.dot_general(
            inputs, hidden_grad, (((0,), (0,)), ((), ())), preferred_element_type=jnp.float32
        )
        * loss_scale
    )


def adapt(inputs, targets, slot_counts, weights, loss_scale):
    positions = jnp.arange(targets[0].shape[2], dtype=jnp.int32)
    valid_mask = (
        (positions[None, None, :] < slot_counts[:, :, None]).astype(jnp.float32).reshape(-1)
    )
    student_part = jnp.zeros(inputs.shape, jnp.float32)
    results = []
    for target, weight_pair in zip(targets, weights):
        expand, project = weight_pair
        hidden = jnp.dot(inputs, expand, preferred_element_type=jnp.float32)
        activated, gelu_slope = gelu_parts(hidden)
        activated = activated.astype(jnp.bfloat16)
        adapted = lax.psum_scatter(
            jnp.dot(activated, project, preferred_element_type=jnp.float32).astype(jnp.bfloat16),
            "mp",
            scatter_dimension=1,
            tiled=True,
        ).astype(jnp.float32)
        target_flat = target.reshape(-1, target.shape[3]).astype(jnp.float32)
        residual = ((adapted - target_flat) * valid_mask[:, None]).astype(jnp.bfloat16)
        back_sum, project_grad = fold_step(
            activated, project, lax.all_gather(residual, "mp", axis=1, tiled=True)
        )
        hidden_grad = (back_sum * gelu_slope).astype(jnp.bfloat16)
        expand_grad = lax.psum_scatter(
            first_term(inputs, hidden_grad, loss_scale).astype(jnp.bfloat16),
            "dp",
            scatter_dimension=0,
            tiled=True,
        ).astype(jnp.float32)
        project_grad = lax.psum_scatter(
            (project_grad * loss_scale).astype(jnp.bfloat16), "dp", scatter_dimension=1, tiled=True
        ).astype(jnp.float32)
        student_part = student_part + lax.dot_general(
            hidden_grad, expand, (((1,), (1,)), ((), ())), preferred_element_type=jnp.float32
        )
        results.append(expand_grad)
        results.append(project_grad)
    return (student_part, results)


def shards(
    student,
    dino_target,
    siglip_target,
    clip_target,
    image_owner,
    patch_count,
    dino_expand,
    dino_project,
    siglip_expand,
    siglip_project,
    clip_expand,
    clip_project,
):
    stores = lax.axis_size("dp")
    store_index = lax.axis_index("dp")
    per_store = dino_target.shape[0]
    patches = dino_target.shape[1]
    slot_total = student.shape[0]
    capacity = slot_total // stores
    owners = image_owner[:, 0]
    store_owner = owners.reshape(stores, per_store)
    counts_store = patch_count.reshape(stores, per_store)
    loss_scale = 1.0 / jnp.sqrt(jnp.sum(patch_count).astype(jnp.float32))
    own_block = lax.dynamic_slice_in_dim(owners, store_index * per_store, per_store)
    sel_store = selection(own_block, jnp.arange(stores, dtype=jnp.int32), capacity)
    picker = sel_store.astype(jnp.bfloat16)
    teachers = (dino_target, siglip_target, clip_target)
    weights = (
        (dino_expand, dino_project),
        (siglip_expand, siglip_project),
        (clip_expand, clip_project),
    )
    outgoing = tuple(
        (
            jnp.einsum("oki,ipf->okpf", picker, teacher, preferred_element_type=jnp.float32).astype(
                jnp.bfloat16
            )
            for teacher in teachers
        )
    )
    targets = jax.tree.map(
        lambda part, own: part.astype(own.dtype),
        lax.all_to_all(for_sending(outgoing), "dp", split_axis=0, concat_axis=0, tiled=True),
        outgoing,
    )
    owner_key = jnp.reshape(store_index, (1,))
    sel_owner = jax.vmap(lambda store_block: selection(store_block, owner_key, capacity)[0])(
        store_owner
    )
    slot_counts = jnp.sum(sel_owner * counts_store[:, None, :], axis=2)
    inputs = student.reshape(-1, student.shape[2])
    student_part, results = adapt(inputs, targets, slot_counts, weights, loss_scale)
    student_grad = lax.psum_scatter(
        student_part.reshape(slot_total, patches, -1).astype(jnp.bfloat16),
        "mp",
        scatter_dimension=2,
        tiled=True,
    )
    return (student_grad, results[0], results[1], results[2], results[3], results[4], results[5])


def solution(mesh):
    return jax.shard_map(
        shards,
        mesh=mesh,
        in_specs=(
            P("dp", None, None),
            P("dp", None, "mp"),
            P("dp", None, "mp"),
            P("dp", None, "mp"),
            P(),
            P(),
            P(None, "mp"),
            P("mp", None),
            P(None, "mp"),
            P("mp", None),
            P(None, "mp"),
            P("mp", None),
        ),
        out_specs=(
            P("dp", None, "mp"),
            P("dp", "mp"),
            P("mp", "dp"),
            P("dp", "mp"),
            P("mp", "dp"),
            P("dp", "mp"),
            P("mp", "dp"),
        ),
        check_vma=False,
    )
```

profile of v0, /device:TPU:0, one launch (start us, length us, event | category | flops | bytes accessed | tf_op | source)
XLA Modules:
  0.0 627.7 jit_solution(5901054520605838002)
XLA Ops:
  7.2 1.5 copy-done
  8.7 3.5 multiply_convert_fusion.1
  12.2 0.8 copy-done.19
  13.0 2.1 convolution_convert_fusion.2
  15.2 1.1 copy-done.6
  16.4 2.2 multiply_convert_fusion.2
  18.6 0.8 copy-done.20
  19.4 2.4 convolution_convert_fusion
  21.9 1.1 copy-done.8
  23.0 1.2 fusion.53
  24.2 1.1 copy-done.22
  25.3 2.8 convolution_convert_fusion.1
  28.1 4.3 copy.50
  33.6 0.8 copy.45
  34.4 7.5 %all-to-all-start.2 = ((bf16[8,6,16,256]{3,2,1,0:T(8,128)(2,1)}), bf16[8,6,16,256]{3,2,1,0:T(8,128)(2,1)S(1)}, u32[]{:S(2)}, u32[]{:S(2)}) async-start(bf16[8,6,16,256]{3,2,1,0:T(8,128)(2,1)} %copy.45), calls=%async_computation.4 | async-start | bytes 786432 | tf_op jit(solution)/shard_map/all_to_all | solution.py:131
  42.7 10.9 %all-to-all-done.2 = bf16[8,6,16,256]{3,2,1,0:T(8,128)(2,1)S(1)} async-done(((bf16[8,6,16,256]{3,2,1,0:T(8,128)(2,1)}), bf16[8,6,16,256]{3,2,1,0:T(8,128)(2,1)S(1)}, u32[]{:S(2)}, u32[]{:S(2)}) %all-to-all-start.2) | async-done | bytes 393248 | tf_op jit(solution)/shard_map/all_to_all | solution.py:131
  53.6 2.0 fusion.27
  56.1 19.8 %all_to_all.15 = bf16[8,6,16,288]{3,2,1,0:T(8,128)(2,1)S(1)} all-to-all(bf16[8,6,16,288]{3,2,1,0:T(8,128)(2,1)S(1)} %copy.42), channel_id=1, replica_groups=mesh['dp'=8,'mp'=4] {'dp'}, dimensions={0} | all-to-all | bytes 884736 | tf_op jit(solution)/shard_map/all_to_all | solution.py:131
  76.0 1.3 copy.43
  77.3 1.1 reduce-scatter.23.cloned.1.call-done
  78.4 2.2 multiply_convert_fusion.4
  80.9 0.9 copy.39
  81.8 5.5 all-to-all-start
  87.3 26.7 %reduce-scatter.31.cloned.1.call-done = bf16[384,768]{1,0:T(8,128)(2,1)} async-done(((bf16[1536,768]{1,0:T(8,128)(2,1)}), bf16[384,768]{1,0:T(8,128)(2,1)}) %reduce-scatter.31.cloned.1.call-update) | async-done | bytes 589840
  114.0 1.4 copy.51
  115.4 1.0 fusion.25
  117.8 17.6 %all-gather.8.cloned.1.call-done = bf16[768,1024]{1,0:T(8,128)(2,1)} async-done(((bf16[768,256]{1,0:T(8,128)(2,1)}), bf16[768,1024]{1,0:T(8,128)(2,1)}) %all-gather.8.cloned.1.call-update) | async-done | bytes 1572880 | tf_op jit(solution)/shard_map/all_gather | solution.py:68
  135.4 2.4 multiply_convert_fusion
  137.8 1.2 copy.60
  139.0 2.9 fusion.11
  142.0 0.8 copy-done.1
  142.8 1.0 fusion.6
  143.8 1.3 copy.58
  145.4 12.3 %all-gather.6.cloned.1.call-done = bf16[768,1152]{0,1:T(8,128)(2,1)} async-done(((bf16[768,288]{0,1:T(8,128)(2,1)}), bf16[768,1152]{0,1:T(8,128)(2,1)}) %all-gather.6.cloned.1.call-update) | async-done | bytes 1769488 | tf_op jit(solution)/shard_map/all_gather | solution.py:68
  157.6 3.5 fusion.4
  161.2 3.2 fusion.10
  164.4 0.8 copy-done.3
  165.3 1.0 fusion.7
  166.2 1.3 copy.56
  167.6 16.2 %all-gather.4.cloned.1.call-done = bf16[768,1536]{1,0:T(8,128)(2,1)} async-done(((bf16[768,384]{1,0:T(8,128)(2,1)}), bf16[768,1536]{1,0:T(8,128)(2,1)}) %all-gather.4.cloned.1.call-update) | async-done | bytes 2359312 | tf_op jit(solution)/shard_map/all_gather | solution.py:68
  183.8 3.9 fusion.9
  187.7 1.0 fusion.8
  188.7 1.3 copy.54
  190.1 4.5 fusion.5
  194.9 2.5 fusion.54
  197.5 1.2 convolution_add_fusion.1
  198.8 2.5 fusion
  201.3 13.9 %copy.52 = bf16[48,16,1280]{1,0,2:T(8,128)(2,1)} copy(bf16[48,16,1280]{2,1,0:T(8,128)(2,1)} %bitcast.87) | data formatting | bytes 3932160
  215.2 18.5 %reshape.148 = bf16[1280,768]{1,0:T(8,128)(2,1)} reshape(bf16[1280,48,16]{2,1,0:T(8,128)(2,1)} %bitcast.84) | data formatting | bytes 3932160
  233.7 16.3 %reduce-scatter.41.cloned.1.call-done = bf16[128,384]{1,0:T(8,128)(2,1)} async-done(((bf16[1024,384]{1,0:T(8,128)(2,1)}), bf16[128,384]{1,0:T(8,128)(2,1)}) %reduce-scatter.41.cloned.1.call-update) | async-done | bytes 98320
  250.0 1.0 copy.61
  251.7 64.0 %reduce-scatter.39.cloned.1.call-done = bf16[160,384]{1,0:T(8,128)(2,1)} async-done(((bf16[1280,384]{1,0:T(8,128)(2,1)}), bf16[160,384]{1,0:T(8,128)(2,1)}) %reduce-scatter.39.cloned.1.call-update) | async-done | bytes 122896
  315.7 1.0 copy.59
  317.5 62.1 %reduce-scatter.29.cloned.1.call-done = bf16[384,144]{0,1:T(8,128)(2,1)} async-done(((bf16[384,1152]{0,1:T(8,128)(2,1)}), bf16[384,144]{0,1:T(8,128)(2,1)}) %reduce-scatter.29.cloned.1.call-update) | async-done | bytes 110608 | tf_op jit(solution)/shard_map/reduce_scatter | solution.py:77
  379.6 1.6 convert_element_type.212
  381.2 64.3 %reduce-scatter.37.cloned.1.call-done = bf16[160,384]{1,0:T(8,128)(2,1)} async-done(((bf16[1280,384]{1,0:T(8,128)(2,1)}), bf16[160,384]{1,0:T(8,128)(2,1)}) %reduce-scatter.37.cloned.1.call-update) | async-done | bytes 122896
  445.6 1.0 copy.57
  447.4 63.9 %reduce-scatter.35.cloned.1.call-done = bf16[160,384]{1,0:T(8,128)(2,1)} async-done(((bf16[1280,384]{1,0:T(8,128)(2,1)}), bf16[160,384]{1,0:T(8,128)(2,1)}) %reduce-scatter.35.cloned.1.call-update) | async-done | bytes 122896
  511.4 1.0 copy.55
  513.2 64.7 %reduce-scatter.27.cloned.1.call-done = bf16[384,192]{0,1:T(8,128)(2,1)} async-done(((bf16[384,1536]{0,1:T(8,128)(2,1)}), bf16[384,192]{0,1:T(8,128)(2,1)}) %reduce-scatter.27.cloned.1.call-update) | async-done | bytes 147472 | tf_op jit(solution)/shard_map/reduce_scatter | solution.py:77
  578.0 1.6 convert_element_type.207
  579.6 30.7 %reduce-scatter.33.cloned.1.call-done = bf16[320,768]{1,0:T(8,128)(2,1)} async-done(((bf16[1280,768]{1,0:T(8,128)(2,1)}), bf16[320,768]{1,0:T(8,128)(2,1)}) %reduce-scatter.33.cloned.1.call-update) | async-done | bytes 491536
  610.3 5.3 reshape.149
  615.6 5.5 copy.53
  (89 shorter events, 7.9 us)
Async XLA Ops:
  7.2 1.6 copy-start
  7.2 46.4 %reduce-scatter.25.cloned.1.call-start = ((), (), s32[]{:S(2)}) async-start(), calls=%async_computation.16 | async-start | bytes 1966080 | tf_op jit(solution)/shard_map/reduce_scatter | solution.py:59
  8.7 4.3 copy-start.17
  12.2 0.8 copy-start.19
  15.2 1.2 copy-start.6
  15.2 63.2 %reduce-scatter.23.cloned.1.call-start = ((), (), s32[]{:S(2)}) async-start(), calls=%async_computation.14 | async-start | bytes 2211840 | tf_op jit(solution)/shard_map/reduce_scatter | solution.py:59
  16.4 3.0 copy-start.15
  18.6 0.8 copy-start.20
  21.8 1.2 copy-start.8
  21.8 92.2 %reduce-scatter.31.cloned.1.call-start = ((), (), s32[]{:S(2)}) async-start(), calls=%async_computation.20 | async-start | bytes 2949120
  23.0 2.3 copy-start.14
  24.2 1.1 copy-start.22
  32.4 0.7 copy-start.13
  32.4 1.0 copy-start.11
  32.4 9.8 %copy-start.12 = (s32[256]{0:T(256)S(1)}, s32[256]{0:T(256)}, u32[]{:S(2)}) copy-start(s32[256]{0:T(256)} %param.17) | copy-start | bytes 3076
  34.4 21.3 %copy-start.9 = (bf16[32,16,288]{2,1,0:T(8,128)(2,1)S(1)}, bf16[32,16,288]{2,1,0:T(8,128)(2,1)}, u32[]{:S(2)}) copy-start(bf16[32,16,288]{2,1,0:T(8,128)(2,1)} %param.14) | copy-start | bytes 884740
  34.4 19.2 %all-to-all-start.2 = ((bf16[8,6,16,256]{3,2,1,0:T(8,128)(2,1)}), bf16[8,6,16,256]{3,2,1,0:T(8,128)(2,1)S(1)}, u32[]{:S(2)}, u32[]{:S(2)}) async-start(bf16[8,6,16,256]{3,2,1,0:T(8,128)(2,1)} %copy.45), calls=%async_computation.4 | async-start | bytes 786432 | tf_op jit(solution)/shard_map/all_to_all | solution.py:131
  41.9 93.5 %all-gather.8.cloned.1.call-start = ((), (), s32[]{:S(2)}) async-start(), calls=%async_computation.17 | async-start | bytes 1966080 | tf_op jit(solution)/shard_map/all_gather | solution.py:68
  55.6 102.0 %all-gather.6.cloned.1.call-start = ((), (), s32[]{:S(2)}) async-start(), calls=%async_computation.15 | async-start | bytes 2211840 | tf_op jit(solution)/shard_map/all_gather | solution.py:68
  77.3 3.2 copy-start.10
  81.8 33.6 %all-to-all-start = ((bf16[8,6,16,384]{3,2,1,0:T(8,128)(2,1)}), bf16[8,6,16,384]{3,2,1,0:T(8,128)(2,1)S(1)}, u32[]{:S(2)}, u32[]{:S(2)}) async-start(bf16[8,6,16,384]{3,2,1,0:T(8,128)(2,1)} %copy.39), calls=%async_computation | async-start | bytes 1179648 | tf_op jit(solution)/shard_map/all_to_all | solution.py:131
  87.3 96.5 %all-gather.4.cloned.1.call-start = ((), (), s32[]{:S(2)}) async-start(), calls=%async_computation.13 | async-start | bytes 2949120 | tf_op jit(solution)/shard_map/all_gather | solution.py:68
  116.4 133.6 %reduce-scatter.41.cloned.1.call-start = ((), (), s32[]{:S(2)}) async-start(), calls=%async_computation.25 | async-start | bytes 884736
  137.8 1.2 copy-start.18
  139.0 176.7 %reduce-scatter.39.cloned.1.call-start = ((), (), s32[]{:S(2)}) async-start(), calls=%async_computation.24 | async-start | bytes 1105920
  142.0 0.8 copy-start.1
  143.8 13.9 %copy-start.21 = (bf16[768,384]{1,0:T(8,128)(2,1)S(1)}, bf16[768,384]{1,0:T(8,128)(2,1)}, u32[]{:S(2)}) copy-start(bf16[768,384]{1,0:T(8,128)(2,1)} %copy-done.20) | copy-start | bytes 1769476
  145.1 16.1 %copy-start.16 = (bf16[384,1152]{1,0:T(8,128)(2,1)S(1)}, bf16[384,1152]{1,0:T(8,128)(2,1)}, u32[]{:S(2)}) copy-start(bf16[384,1152]{1,0:T(8,128)(2,1)} %param.21) | copy-start | bytes 2654212
  145.1 234.5 %reduce-scatter.29.cloned.1.call-start = ((), (), s32[]{:S(2)}) async-start(), calls=%async_computation.19 | async-start | bytes 995328 | tf_op jit(solution)/shard_map/reduce_scatter | solution.py:77
  161.2 284.4 %reduce-scatter.37.cloned.1.call-start = ((), (), s32[]{:S(2)}) async-start(), calls=%async_computation.23 | async-start | bytes 1105920
  164.4 0.8 copy-start.3
  167.6 343.8 %reduce-scatter.35.cloned.1.call-start = ((), (), s32[]{:S(2)}) async-start(), calls=%async_computation.22 | async-start | bytes 1105920
  190.0 387.9 %reduce-scatter.27.cloned.1.call-start = ((), (), s32[]{:S(2)}) async-start(), calls=%async_computation.18 | async-start | bytes 1327104 | tf_op jit(solution)/shard_map/reduce_scatter | solution.py:77
  194.6 2.8 copy-start.4
  194.6 415.7 %reduce-scatter.33.cloned.1.call-start = ((), (), s32[]{:S(2)}) async-start(), calls=%async_computation.21 | async-start | bytes 2457600
  194.9 2.5 copy-start.7
  197.4 1.3 copy-start.2
  197.4 1.4 copy-start.5
Sparse Core Ops, SparseCore 0:
  15.3 30.8 reduce-scatter.24
  49.0 29.3 reduce-scatter.22
  80.9 33.0 reduce-scatter.30
  115.5 19.8 all-gather.7
  136.8 20.7 all-gather.5
  159.7 24.0 all-gather.3
  187.4 62.5 reduce-scatter.40
  253.3 62.2 reduce-scatter.38
  319.5 60.1 reduce-scatter.28
  383.2 62.3 reduce-scatter.36
  448.9 62.3 reduce-scatter.34
  515.0 62.9 reduce-scatter.26
  580.7 29.5 reduce-scatter.32
where the time goes:
time: 629 us; the launch traced here: 628 us
  waiting for transfers between devices  451 us (72%)
  local copies, waits for them, and re-layouts  72.9 us (12%)
  matrix products  44.7 us (7%)
  blocking collectives  19.8 us (3%)
  between operations  14.9 us (2%)
  starting transfers between devices  13.9 us (2%)
  other arithmetic  10.6 us (2%)
    unnamed x19, waiting for transfers between devices  266 us
    reduce_scatter x2, waiting for transfers between devices, adapt(): lax.psum_scatter((project_grad * loss_scale).astype(jnp.bfloat16), 'dp',...  127 us
    unnamed x63, local copies, waits for them, and re-layouts  69.4 us
    all_gather x3, waiting for transfers between devices, adapt(): lax.all_gather(residual, 'mp', axis=1, tiled=True)  46 us
    all_to_all x1, blocking collectives, shards(): lax.all_to_all(for_sending(outgoing), 'dp', split_axis=0, concat_axis=0,...  19.8 us
    all_to_all x2, starting transfers between devices, shards(): lax.all_to_all(for_sending(outgoing), 'dp', split_axis=0, concat_axis=0,...  13 us
  transfers between devices with their start and end apart: 15, of which 13 were waited for; matrix products, arithmetic and copies ran while one was open for 16% of the time, Pallas kernels for 0%

commit v1 on v0

--- a/solution.py
+++ b/solution.py
@@ -1,7 +1,15 @@
+import functools
+
 import jax
 import jax.numpy as jnp
 from jax import lax
+from jax.experimental import pallas as pl
+from jax.experimental.pallas import tpu as pltpu
 from jax.sharding import PartitionSpec as P
+
+MESH = pl.DeviceIdType.MESH
+F32 = jnp.float32
+BF16 = jnp.bfloat16
 
 
 def for_sending(value):
@@ -147,9 +155,374 @@
     return (student_grad, results[0], results[1], results[2], results[3], results[4], results[5])
 
 
+def nn(a, b):
+    return lax.dot_general(a, b, (((1,), (0,)), ((), ())), preferred_element_type=F32)
+
+
+def nt(a, b):
+    return lax.dot_general(a, b, (((1,), (1,)), ((), ())), preferred_element_type=F32)
+
+
+def tn(a, b):
+    return lax.dot_general(a, b, (((0,), (0,)), ((), ())), preferred_element_type=F32)
+
+
+def rows_at(index, size):
+    return pl.ds(pl.multiple_of(index * size, 16), size)
+
+
+def fused_kernel(names, orders, *refs):
+    r = dict(zip(names, refs))
+    dp, mp = lax.axis_index("dp"), lax.axis_index("mp")
+    x, core = mp // 2, mp % 2
+    sibling = mp + 1 - 2 * core
+    across = mp + 2 - 4 * x
+    n_dp, n_mp = 8, 4
+    sent = []
+    numbers = iter(range(r["ssem"].shape[0]))
+
+    def send(source, landing, device):
+        number = next(numbers)
+        copy = pltpu.make_async_remote_copy(
+            src_ref=source,
+            dst_ref=landing,
+            send_sem=r["ssem"].at[number],
+            recv_sem=r["rsem"].at[number],
+            device_id=device,
+            device_id_type=MESH,
+        )
+        copy.start()
+        sent.append(copy)
+        return copy
+
+    dp_peers = [lax.rem(dp + k, n_dp) for k in range(1, n_dp)]
+    barrier = pltpu.get_barrier_semaphore()
+    for peer in dp_peers:
+        pl.semaphore_signal(barrier, inc=1, device_id=(peer, mp), device_id_type=MESH)
+    for peer in (sibling, across):
+        pl.semaphore_signal(barrier, inc=1, device_id=(dp, peer), device_id_type=MESH)
+    pl.semaphore_wait(barrier, n_dp + 1)
+
+    xs, xr, xt = r["xs"], r["xr"], r["xt"]
+    quarter = xt.shape[0] // n_mp
+    slot_rows, row_total = xr.shape[0] * xr.shape[1], xt.shape[1]
+    arrivals = [send(xs.at[peer], xr.at[dp], (peer, mp)) for peer in dp_peers]
+    xr[dp] = xs[dp]
+    picked = lax.broadcasted_iota(jnp.int32, (slot_rows, row_total), 0) == r["place"][...]
+    r["sel"][...] = picked.astype(F32).astype(BF16)
+    for copy in arrivals:
+        copy.wait_recv()
+    mine = rows_at(mp, quarter)
+    theirs = rows_at(across, quarter)
+    xt[mine, :] = tn(xr[...].reshape(slot_rows, quarter), r["sel"][...]).astype(BF16)
+    to_sibling = send(xt.at[mine, :], xt.at[mine, :], (dp, sibling))
+    to_across = send(xt.at[mine, :], xt.at[mine, :], (dp, across))
+    to_across.wait_recv()
+    forward = send(xt.at[theirs, :], xt.at[theirs, :], (dp, sibling))
+    to_sibling.wait_recv()
+    forward.wait_recv()
+
+    teachers = range(3)
+    core_copy, x_copy, gather = {}, {}, {}
+
+    def first_half(t):
+        expand, project_t = r[f"expand{t}"], r[f"project_t{t}"]
+        hidden = tn(expand[...], xt[...])
+        cdf = 0.5 * (1.0 + lax.erf(hidden * 0.7071067811865476))
+        density = jnp.exp(-0.5 * hidden * hidden) * 0.3989422804014327
+        r[f"slope{t}"][...] = cdf + hidden * density
+        r[f"act{t}"][...] = (hidden * cdf).astype(BF16)
+        part = r[f"part{t}"]
+        width = part.shape[2]
+
+        def block(j, carry):
+            part[j % 2, j // 2] = nn(
+                project_t[rows_at(j, width), :], r[f"act{t}"][...]
+            ).astype(BF16)
+            return carry
+
+        lax.fori_loop(0, n_mp, block, 0)
+        core_copy[t] = send(part.at[1 - core], r[f"from_core{t}"], (dp, sibling))
+
+    def to_x(t):
+        part, landed = r[f"part{t}"], r[f"from_core{t}"]
+        core_copy[t].wait_recv()
+        part[core, 1 - x] = (
+            part[core, 1 - x].astype(F32) + landed[1 - x].astype(F32)
+        ).astype(BF16)
+        x_copy[t] = send(part.at[core, 1 - x], r[f"from_x{t}"], (dp, across))
+
+    def residual(t):
+        part, landed, res = r[f"part{t}"], r[f"from_core{t}"], r[f"res{t}"]
+        width = part.shape[2]
+        own = part[core, x].astype(F32) + landed[x].astype(F32)
+        x_copy[t].wait_recv()
+        adapted = own + r[f"from_x{t}"][...].astype(F32)
+        here = rows_at(mp, width)
+        res[here, :] = ((adapted - r[f"target{t}"][...].astype(F32)) * r["valid"][...]).astype(BF16)
+        near = send(res.at[here, :], res.at[here, :], (dp, sibling))
+        far = send(res.at[here, :], res.at[here, :], (dp, across))
+        gather[t] = (near, far)
+
+    def pass_on(t):
+        res = r[f"res{t}"]
+        there = rows_at(across, r[f"part{t}"].shape[2])
+        near, far = gather[t]
+        far.wait_recv()
+        gather[t] = (near, send(res.at[there, :], res.at[there, :], (dp, sibling)))
+
+    def bit_of(index, bit):
+        return (index // bit) % 2
+
+    def partner(bit):
+        return dp + bit - 2 * bit * bit_of(dp, bit)
+
+    stage = {}
+
+    def start_reduce(i):
+        total, order = r[f"sum{i}"], orders[i]
+        stage[i] = send(
+            total.at[1 - bit_of(dp, order[0])], r[f"first{i}"], (partner(order[0]), mp)
+        )
+
+    def second(i):
+        total, landed, order = r[f"sum{i}"], r[f"first{i}"], orders[i]
+        own = bit_of(dp, order[0])
+        stage[i].wait_recv()
+
+        def block(k, carry):
+            a, b = k // 2, k % 2
+            total[own, a, b] = (
+                total[own, a, b].astype(F32) + landed[a, b].astype(F32)
+            ).astype(BF16)
+            return carry
+
+        lax.fori_loop(0, 4, block, 0)
+        stage[i] = send(
+            total.at[own, 1 - bit_of(dp, order[1])], r[f"next{i}"], (partner(order[1]), mp)
+        )
+
+    def third(i):
+        total, landed, order = r[f"sum{i}"], r[f"next{i}"], orders[i]
+        own, mid = bit_of(dp, order[0]), bit_of(dp, order[1])
+        stage[i].wait_recv()
+
+        def block(k, carry):
+            total[own, mid, k] = (
+                total[own, mid, k].astype(F32) + landed[k].astype(F32)
+            ).astype(BF16)
+            return carry
+
+        lax.fori_loop(0, 2, block, 0)
+        stage[i] = send(
+            total.at[own, mid, 1 - bit_of(dp, order[2])], r[f"last{i}"], (partner(order[2]), mp)
+        )
+
+    def finish(i):
+        total, order = r[f"sum{i}"], orders[i]
+        own = [bit_of(dp, bit) for bit in order]
+        stage[i].wait_recv()
+        r[f"out{i}"][...] = (
+            total[own[0], own[1], own[2]].astype(F32) + r[f"last{i}"][...].astype(F32)
+        ) * r["scale"][...]
+
+    def grads(t):
+        res, act, grad = r[f"res{t}"], r[f"act{t}"], r[f"grad{t}"]
+        near, forwarded = gather[t]
+        near.wait_recv()
+        forwarded.wait_recv()
+        for i, left, right in ((2 * t, res, act), (2 * t + 1, xt, grad)):
+            total, order = r[f"sum{i}"], orders[i]
+            size = total.shape[3]
+            if right is grad:
+                back = nn(r[f"project{t}"][...], res[...])
+                grad[...] = (back * r[f"slope{t}"][...]).astype(BF16)
+
+            def block(k, carry):
+                place = [bit_of(k, bit) for bit in order]
+                total[place[0], place[1], place[2]] = nt(
+                    left[rows_at(k, size), :], right[...]
+                ).astype(BF16)
+                return carry
+
+            lax.fori_loop(0, n_dp, block, 0)
+            start_reduce(i)
+
+    first_half(0)
+    first_half(1)
+    to_x(0)
+    first_half(2)
+    to_x(1)
+    residual(0)
+    to_x(2)
+    residual(1)
+    pass_on(0)
+    grads(0)
+    residual(2)
+    pass_on(1)
+    pass_on(2)
+    grads(1)
+    second(0)
+    second(1)
+    grads(2)
+
+    sp = r["sp"]
+
+    def block(j, carry):
+        sp[j % 2, j // 2] = sum(
+            nn(r[f"expand{t}"][rows_at(j, quarter), :], r[f"grad{t}"][...]) for t in teachers
+        ).astype(BF16)
+        return carry
+
+    lax.fori_loop(0, n_mp, block, 0)
+    core_copy["s"] = send(sp.at[1 - core], r["sp_core"], (dp, sibling))
+    third(0)
+    second(2)
+    third(1)
+    core_copy["s"].wait_recv()
+    sp[core, 1 - x] = (
+        sp[core, 1 - x].astype(F32) + r["sp_core"][1 - x].astype(F32)
+    ).astype(BF16)
+    x_copy["s"] = send(sp.at[core, 1 - x], r["sp_x"], (dp, across))
+    second(3)
+    third(2)
+    finish(0)
+    own = sp[core, x].astype(F32) + r["sp_core"][x].astype(F32)
+    x_copy["s"].wait_recv()
+    summed = (own + r["sp_x"][...].astype(F32)).astype(BF16)
+    placed = nt(r["sel"][...], summed).astype(BF16)
+    r["home"][...] = placed.reshape(r["home"].shape)
+    returns = [
+        send(r["home"].at[peer], r["student_out"].at[dp], (peer, mp)) for peer in dp_peers
+    ]
+    r["student_out"][dp] = r["home"][dp]
+    second(4)
+    third(3)
+    finish(1)
+    second(5)
+    third(4)
+    finish(2)
+    third(5)
+    finish(3)
+    finish(4)
+    finish(5)
+    for copy in returns:
+        copy.wait_recv()
+    for copy in sent:
+        copy.wait_send()
+
+
+def fused(
+    student,
+    dino_target,
+    siglip_target,
+    clip_target,
+    image_owner,
+    patch_count,
+    dino_expand,
+    dino_project,
+    siglip_expand,
+    siglip_project,
+    clip_expand,
+    clip_project,
+):
+    stores, groups = lax.axis_size("dp"), lax.axis_size("mp")
+    dp, mp = lax.axis_index("dp"), lax.axis_index("mp")
+    per_store, patches = dino_target.shape[0], dino_target.shape[1]
+    capacity = student.shape[0] // stores
+    width = student.shape[2]
+    quarter = width // groups
+    rows = per_store * patches
+    owners = lax.dynamic_slice_in_dim(image_owner[:, 0], dp * per_store, per_store)
+    counts = lax.dynamic_slice_in_dim(patch_count, dp * per_store, per_store)
+    index = jnp.arange(per_store, dtype=jnp.int32)
+    earlier = (index[None, :] < index[:, None]) & (owners[None, :] == owners[:, None])
+    slot = owners * capacity + jnp.sum(earlier.astype(jnp.int32), axis=1)
+    patch = jnp.arange(patches, dtype=jnp.int32)
+    place = (slot[:, None] * patches + patch[None, :]).reshape(1, rows)
+    valid = (patch[None, :] < counts[:, None]).astype(F32).reshape(1, rows)
+    loss_scale = 1.0 / jnp.sqrt(jnp.sum(patch_count).astype(F32))
+    hidden = dino_expand.shape[1]
+    scale = jnp.broadcast_to(loss_scale, (1, hidden))
+    xs = lax.dynamic_slice_in_dim(
+        student.reshape(stores, capacity * patches, width), mp * quarter, quarter, axis=2
+    )
+    expands = (dino_expand, siglip_expand, clip_expand)
+    projects = (dino_project, siglip_project, clip_project)
+    targets = (dino_target, siglip_target, clip_target)
+
+    inputs = {"xs": xs, "place": place, "valid": valid, "scale": scale}
+    outputs = {"student_out": jax.ShapeDtypeStruct(xs.shape, BF16)}
+    scratch = {
+        "ssem": pltpu.SemaphoreType.DMA((52,)),
+        "rsem": pltpu.SemaphoreType.DMA((52,)),
+        "xr": pltpu.VMEM(xs.shape, BF16),
+        "home": pltpu.VMEM(xs.shape, BF16),
+        "xt": pltpu.VMEM((width, rows), BF16),
+        "sel": pltpu.VMEM((stores * capacity * patches, rows), BF16),
+        "sp": pltpu.VMEM((2, 2, quarter, rows), BF16),
+        "sp_core": pltpu.VMEM((2, quarter, rows), BF16),
+        "sp_x": pltpu.VMEM((quarter, rows), BF16),
+    }
+    orders = []
+    for t, (target, expand, project) in enumerate(zip(targets, expands, projects)):
+        columns = target.shape[2]
+        features = project.shape[1]
+        inputs[f"target{t}"] = target.reshape(rows, columns).T
+        inputs[f"expand{t}"] = expand
+        inputs[f"project{t}"] = project
+        inputs[f"project_t{t}"] = project.T
+        scratch[f"slope{t}"] = pltpu.VMEM((hidden, rows), F32)
+        scratch[f"act{t}"] = pltpu.VMEM((hidden, rows), BF16)
+        scratch[f"grad{t}"] = pltpu.VMEM((hidden, rows), BF16)
+        scratch[f"part{t}"] = pltpu.VMEM((2, 2, columns, rows), BF16)
+        scratch[f"from_core{t}"] = pltpu.VMEM((2, columns, rows), BF16)
+        scratch[f"from_x{t}"] = pltpu.VMEM((columns, rows), BF16)
+        scratch[f"res{t}"] = pltpu.VMEM((features, rows), BF16)
+        for i, size in ((2 * t, features // stores), (2 * t + 1, width // stores)):
+            outputs[f"out{i}"] = jax.ShapeDtypeStruct((size, hidden), F32)
+            scratch[f"sum{i}"] = pltpu.VMEM((2, 2, 2, size, hidden), BF16)
+            scratch[f"first{i}"] = pltpu.VMEM((2, 2, size, hidden), BF16)
+            scratch[f"next{i}"] = pltpu.VMEM((2, size, hidden), BF16)
+            scratch[f"last{i}"] = pltpu.VMEM((size, hidden), BF16)
+            orders.append((2, 1, 4) if i == 2 else (1, 2, 4))
+    names = list(inputs) + list(outputs) + list(scratch)
+    vmem = pl.BlockSpec(memory_space=pltpu.VMEM)
+    features = sum(project.shape[1] for project in projects)
+    results = pl.pallas_call(
+        functools.partial(fused_kernel, names, orders),
+        out_shape=tuple(outputs.values()),
+        in_specs=[vmem] * len(inputs),
+        out_specs=tuple([vmem] * len(outputs)),
+        scratch_shapes=list(scratch.values()),
+        compiler_params=pltpu.CompilerParams(
+            collective_id=0, has_side_effects=True, vmem_limit_bytes=60 * 1024 * 1024
+        ),
+        cost_estimate=pl.CostEstimate(
+            flops=6 * rows * hidden * (features + 3 * width),
+            bytes_accessed=16 * 1024 * 1024,
+            transcendentals=6 * rows * hidden,
+        ),
+    )(*inputs.values())
+    student_grad = results[0].reshape(student.shape[0], patches, quarter)
+    return (
+        student_grad,
+        results[2],
+        results[1].T,
+        results[4],
+        results[3].T,
+        results[6],
+        results[5].T,
+    )
+
+
+def kernel_fits(mesh):
+    return mesh.shape["dp"] == 8 and mesh.shape["mp"] == 4
+
+
 def solution(mesh):
     return jax.shard_map(
-        shards,
+        fused if kernel_fits(mesh) else shards,
         mesh=mesh,
         in_specs=(
             P("dp", None, None),

time: 629 us -> 195 us (0.31)
  waiting for transfers between devices: 451 us -> 0 us
  Pallas kernels: 0 us -> 166 us
  local copies, waits for them, and re-layouts: 72.9 us -> 24.3 us
  matrix products: 44.7 us -> 0 us
  blocking collectives: 19.8 us -> 0 us
  starting transfers between devices: 13.9 us -> 0 us
  between operations: 14.9 us -> 1.4 us
  other arithmetic: 10.6 us -> 2.51 us
    unnamed x19 -> x0, waiting for transfers between devices: 266 us -> none
    pallas_call x0 -> x1, Pallas kernels: none -> 166 us  [fused(): pl.pallas_call(functools.partial(fused_kernel, names, orders), out_shape=...]
    reduce_scatter x4 -> x0, waiting for transfers between devices: 128 us -> none  [the longest x2 127 us: adapt(): lax.psum_scatter((project_grad * loss_scale).astype(jnp.bfloat16), 'dp',...]
    unnamed x63 -> x22, local copies, waits for them, and re-layouts: 69.4 us -> 14.3 us
    all_gather x3 -> x0, waiting for transfers between devices: 46 us -> none  [adapt(): lax.all_gather(residual, 'mp', axis=1, tiled=True)]
    dot_general x21 -> x0, matrix products: 44.7 us -> none  [the longest x3 10.4 us: fold_step(): lax.dot_general(activated, segment, (((0,), (0,)), ((), ())), preferred_e...]
    all_to_all x1 -> x0, blocking collectives: 19.8 us -> none  [shards(): lax.all_to_all(for_sending(outgoing), 'dp', split_axis=0, concat_axis=0,...]
    all_to_all x2 -> x0, starting transfers between devices: 13 us -> none  [shards(): lax.all_to_all(for_sending(outgoing), 'dp', split_axis=0, concat_axis=0,...]
  transfers between devices with their start and end apart: 15 -> 0, of which waited for: 13 -> 0; matrix products, arithmetic and copies ran while one was open for 16% -> 0% of each run, Pallas kernels for 0% -> 0%
where the time goes in v1:
time: 195 us
  Pallas kernels  166 us (85%)
  local copies, waits for them, and re-layouts  24.3 us (12%)
  other arithmetic  2.51 us (1%)
    pallas_call x1, Pallas kernels, fused(): pl.pallas_call(functools.partial(fused_kernel, names, orders), out_shape=...  166 us
    unnamed x22, local copies, waits for them, and re-layouts  14.3 us
    reshape x3, local copies, waits for them, and re-layouts, fused(): inputs[f'target{t}'] = target.reshape(rows, columns).T  5.58 us

profile of v1, /device:TPU:0, one launch (start us, length us, event | category | flops | bytes accessed | tf_op | source)
XLA Modules:
  0.0 194.5 jit_solution(9396720689590954156)
XLA Ops:
  0.6 0.0 copy-start
  0.7 1.5 reduce_sum.22
  2.8 0.0 copy-done
  2.8 0.7 fusion.4
  3.5 0.2 convert_reduce_fusion
  3.7 0.7 fusion.3
  4.5 0.8 dynamic_slice.11
  5.2 0.6 broadcast_in_dim.2.refs_3_
  5.8 0.1 fusion.1
  5.8 0.7 reshape.92.refs_2_
  6.5 0.1 iota_add_fusion
  6.6 0.7 add.45.refs_1_
  7.2 1.8 copy.37
  9.0 1.9 copy.35
  10.9 1.9 copy.33
  12.8 1.1 constant_dynamic-slice_fusion.1.refs_0_
  13.9 0.0 copy-start.1
  13.9 2.4 %copy.38 = bf16[384,1024]{0,1:T(8,128)(2,1)} copy(bf16[384,1024]{1,0:T(8,128)(2,1)} %refs_14_.1) | data formatting | bytes 1572864 | tf_op args[11]
  16.3 2.2 %copy.36 = bf16[384,1152]{0,1:T(8,128)(2,1)} copy(bf16[384,1152]{1,0:T(8,128)(2,1)} %refs_10_.1) | data formatting | bytes 1769472 | tf_op args[9]
  18.5 0.0 copy-done.1
  18.6 1.4 copy.34
  19.9 166.3 %shard_map.171 = (bf16[8,96,320]{2,1,0:T(8,128)(2,1)}, f32[192,384]{1,0:T(8,128)}, f32[160,384]{1,0:T(8,128)}, f32[144,384]{1,0:T(8,128)}, f32[160,384]{1,0:T(8,...) custom-call(bf16[8,96,320]{2,1,0:T(8,128)(2,1)} %constant_dynamic-slice_fusion.1.refs_0_, s32[1,512]{1,0:T(1,128)} %add.45.refs_1_, ...), custom_call_target="tpu_custom_call" | custom-call | flops 8908701696 | bytes 16777216 | tf_op jit(solution)/shard_map/pallas_call | solution.py:492
  186.3 0.0 copy-start.2
  186.3 0.0 copy-start.4
  186.3 0.0 copy-start.5
  186.3 0.0 copy-start.3
  186.3 1.8 copy.39
  188.2 1.9 copy.46
  190.1 1.7 copy.47
  191.7 0.0 copy-done.2
  191.7 0.7 copy.48
  192.5 0.0 copy-done.4
  192.5 0.7 copy.49
  193.2 0.0 copy-done.5
  193.2 0.7 copy.50
  193.8 0.0 copy-done.3
  193.8 0.7 copy.51
Async XLA Ops:
  0.6 2.2 %copy-start = (bf16[48,16,1280]{2,1,0:T(8,128)(2,1)S(1)}, bf16[48,16,1280]{2,1,0:T(8,128)(2,1)}, u32[]{:S(2)}) copy-start(bf16[48,16,1280]{2,1,0:T(8,128)(2,1)} %param.12) | copy-start | bytes 5898244
  13.9 4.6 %copy-start.1 = (bf16[384,1536]{1,0:T(8,128)(2,1)S(1)}, bf16[384,1536]{1,0:T(8,128)(2,1)}, u32[]{:S(2)}) copy-start(bf16[384,1536]{1,0:T(8,128)(2,1)} %refs_6_.1) | copy-start | bytes 3538948
  186.3 5.4 %copy-start.2 = (f32[192,384]{1,0:T(8,128)S(1)}, f32[192,384]{1,0:T(8,128)}, u32[]{:S(2)}) copy-start(f32[192,384]{1,0:T(8,128)} %get-tuple-element.16) | copy-start | bytes 884740
  186.3 6.2 %copy-start.4 = (f32[160,384]{1,0:T(8,128)S(1)}, f32[160,384]{1,0:T(8,128)}, u32[]{:S(2)}) copy-start(f32[160,384]{1,0:T(8,128)} %get-tuple-element.52) | copy-start | bytes 737284
  186.3 6.8 %copy-start.5 = (f32[144,384]{1,0:T(8,128)S(1)}, f32[144,384]{1,0:T(8,128)}, u32[]{:S(2)}) copy-start(f32[144,384]{1,0:T(8,128)} %get-tuple-element.18) | copy-start | bytes 663556
  186.3 7.5 %copy-start.3 = (f32[160,384]{1,0:T(8,128)S(1)}, f32[160,384]{1,0:T(8,128)}, u32[]{:S(2)}) copy-start(f32[160,384]{1,0:T(8,128)} %get-tuple-element.54) | copy-start | bytes 737284

commit v2 on v1

--- a/solution.py
+++ b/solution.py
@@ -171,7 +171,7 @@
     return pl.ds(pl.multiple_of(index * size, 16), size)
 
 
-def fused_kernel(names, orders, *refs):
+def fused_kernel(names, names_loaded, orders, capacity, patches, *refs):
     r = dict(zip(names, refs))
     dp, mp = lax.axis_index("dp"), lax.axis_index("mp")
     x, core = mp // 2, mp % 2
@@ -195,6 +195,11 @@
         sent.append(copy)
         return copy
 
+    loads = {}
+    for number, name in enumerate(names_loaded):
+        loads[name] = pltpu.make_async_copy(r[name + "_hbm"], r[name], r["lsem"].at[number])
+        loads[name].start()
+
     dp_peers = [lax.rem(dp + k, n_dp) for k in range(1, n_dp)]
     barrier = pltpu.get_barrier_semaphore()
     for peer in dp_peers:
@@ -208,8 +213,37 @@
     slot_rows, row_total = xr.shape[0] * xr.shape[1], xt.shape[1]
     arrivals = [send(xs.at[peer], xr.at[dp], (peer, mp)) for peer in dp_peers]
     xr[dp] = xs[dp]
-    picked = lax.broadcasted_iota(jnp.int32, (slot_rows, row_total), 0) == r["place"][...]
+
+    owners, counts = r["owners"][...], r["counts"][...]
+    images = owners.shape[1]
+    per_store = row_total // patches
+    first_image = dp * per_store
+    image = lax.broadcasted_iota(jnp.int32, (images, row_total), 0) - first_image
+    column = lax.broadcasted_iota(jnp.int32, (images, row_total), 1)
+    at_column = column // patches
+    same = (image == at_column).astype(F32).astype(BF16)
+    before = ((image >= 0) & (image < at_column)).astype(F32).astype(BF16)
+    padded = jnp.broadcast_to(owners, (8, images))
+    owner_of = nn(padded.astype(F32).astype(BF16), same)
+    count_of = nn(jnp.broadcast_to(counts, (8, images)).astype(F32).astype(BF16), same)
+    named = lax.broadcasted_iota(jnp.int32, (n_dp, images), 0) == padded
+    ranks = nn(named.astype(F32).astype(BF16), before)
+    ours = lax.broadcasted_iota(jnp.int32, (n_dp, row_total), 0) == owner_of.astype(jnp.int32)
+    rank = jnp.sum(jnp.where(ours, ranks, 0.0), axis=0, keepdims=True)
+    patch = column[:1] - at_column[:1] * patches
+    slot = owner_of[:1].astype(jnp.int32) * capacity + rank.astype(jnp.int32)
+    r["valid"][...] = (patch < count_of[:1].astype(jnp.int32)).astype(F32)
+    total = jnp.sum(counts.astype(F32), axis=1, keepdims=True)
+    r["scale"][...] = jnp.broadcast_to(1.0 / jnp.sqrt(total), r["scale"].shape)
+    place = slot * patches + patch
+    picked = lax.broadcasted_iota(jnp.int32, (slot_rows, row_total), 0) == place
     r["sel"][...] = picked.astype(F32).astype(BF16)
+    for name in names_loaded:
+        loads[name].wait()
+    for t in range(3):
+        r[f"expand_t{t}"][...] = r[f"expand{t}"][...].T
+        r[f"project_t{t}"][...] = r[f"project{t}"][...].T
+        r[f"target_t{t}"][...] = r[f"target{t}"][...].T
     for copy in arrivals:
         copy.wait_recv()
     mine = rows_at(mp, quarter)
@@ -226,8 +260,8 @@
     core_copy, x_copy, gather = {}, {}, {}
 
     def first_half(t):
-        expand, project_t = r[f"expand{t}"], r[f"project_t{t}"]
-        hidden = tn(expand[...], xt[...])
+        project_t = r[f"project_t{t}"]
+        hidden = nn(r[f"expand_t{t}"][...], xt[...])
         cdf = 0.5 * (1.0 + lax.erf(hidden * 0.7071067811865476))
         density = jnp.exp(-0.5 * hidden * hidden) * 0.3989422804014327
         r[f"slope{t}"][...] = cdf + hidden * density
@@ -259,7 +293,7 @@
         x_copy[t].wait_recv()
         adapted = own + r[f"from_x{t}"][...].astype(F32)
         here = rows_at(mp, width)
-        res[here, :] = ((adapted - r[f"target{t}"][...].astype(F32)) * r["valid"][...]).astype(BF16)
+        res[here, :] = ((adapted - r[f"target_t{t}"][...].astype(F32)) * r["valid"][...]).astype(BF16)
         near = send(res.at[here, :], res.at[here, :], (dp, sibling))
         far = send(res.at[here, :], res.at[here, :], (dp, across))
         gather[t] = (near, far)
@@ -322,9 +356,10 @@
         total, order = r[f"sum{i}"], orders[i]
         own = [bit_of(dp, bit) for bit in order]
         stage[i].wait_recv()
-        r[f"out{i}"][...] = (
+        summed = (
             total[own[0], own[1], own[2]].astype(F32) + r[f"last{i}"][...].astype(F32)
         ) * r["scale"][...]
+        r[f"out{i}"][...] = summed.T if i % 2 == 0 else summed
 
     def grads(t):
         res, act, grad = r[f"res{t}"], r[f"act{t}"], r[f"grad{t}"]
@@ -339,29 +374,29 @@
                 grad[...] = (back * r[f"slope{t}"][...]).astype(BF16)
 
             def block(k, carry):
-                place = [bit_of(k, bit) for bit in order]
-                total[place[0], place[1], place[2]] = nt(
-                    left[rows_at(k, size), :], right[...]
-                ).astype(BF16)
+                both = nt(left[rows_at(k, 2 * size), :], right[...]).astype(BF16)
+                for low in (0, 1):
+                    at = [bit_of(2 * k + low, bit) for bit in order]
+                    total[at[0], at[1], at[2]] = both[low * size : (low + 1) * size]
                 return carry
 
-            lax.fori_loop(0, n_dp, block, 0)
+            lax.fori_loop(0, n_dp // 2, block, 0)
             start_reduce(i)
 
     first_half(0)
+    to_x(0)
     first_half(1)
-    to_x(0)
+    residual(0)
+    to_x(1)
     first_half(2)
-    to_x(1)
-    residual(0)
+    pass_on(0)
+    residual(1)
     to_x(2)
-    residual(1)
-    pass_on(0)
     grads(0)
+    pass_on(1)
     residual(2)
-    pass_on(1)
+    grads(1)
     pass_on(2)
-    grads(1)
     second(0)
     second(1)
     grads(2)
@@ -427,35 +462,33 @@
     clip_project,
 ):
     stores, groups = lax.axis_size("dp"), lax.axis_size("mp")
-    dp, mp = lax.axis_index("dp"), lax.axis_index("mp")
+    mp = lax.axis_index("mp")
     per_store, patches = dino_target.shape[0], dino_target.shape[1]
     capacity = student.shape[0] // stores
     width = student.shape[2]
     quarter = width // groups
     rows = per_store * patches
-    owners = lax.dynamic_slice_in_dim(image_owner[:, 0], dp * per_store, per_store)
-    counts = lax.dynamic_slice_in_dim(patch_count, dp * per_store, per_store)
-    index = jnp.arange(per_store, dtype=jnp.int32)
-    earlier = (index[None, :] < index[:, None]) & (owners[None, :] == owners[:, None])
-    slot = owners * capacity + jnp.sum(earlier.astype(jnp.int32), axis=1)
-    patch = jnp.arange(patches, dtype=jnp.int32)
-    place = (slot[:, None] * patches + patch[None, :]).reshape(1, rows)
-    valid = (patch[None, :] < counts[:, None]).astype(F32).reshape(1, rows)
-    loss_scale = 1.0 / jnp.sqrt(jnp.sum(patch_count).astype(F32))
     hidden = dino_expand.shape[1]
-    scale = jnp.broadcast_to(loss_scale, (1, hidden))
     xs = lax.dynamic_slice_in_dim(
         student.reshape(stores, capacity * patches, width), mp * quarter, quarter, axis=2
     )
-    expands = (dino_expand, siglip_expand, clip_expand)
-    projects = (dino_project, siglip_project, clip_project)
-    targets = (dino_target, siglip_target, clip_target)
-
-    inputs = {"xs": xs, "place": place, "valid": valid, "scale": scale}
+    expands = (clip_expand, siglip_expand, dino_expand)
+    projects = (clip_project, siglip_project, dino_project)
+    targets = (clip_target, siglip_target, dino_target)
+
+    inputs = {
+        "xs": xs,
+        "owners": image_owner.reshape(1, -1),
+        "counts": patch_count.reshape(1, -1),
+    }
+    loaded = {}
     outputs = {"student_out": jax.ShapeDtypeStruct(xs.shape, BF16)}
     scratch = {
         "ssem": pltpu.SemaphoreType.DMA((52,)),
         "rsem": pltpu.SemaphoreType.DMA((52,)),
+        "lsem": pltpu.SemaphoreType.DMA((9,)),
+        "valid": pltpu.VMEM((1, rows), F32),
+        "scale": pltpu.VMEM((1, hidden), F32),
         "xr": pltpu.VMEM(xs.shape, BF16),
         "home": pltpu.VMEM(xs.shape, BF16),
         "xt": pltpu.VMEM((width, rows), BF16),
@@ -468,10 +501,12 @@
     for t, (target, expand, project) in enumerate(zip(targets, expands, projects)):
         columns = target.shape[2]
         features = project.shape[1]
-        inputs[f"target{t}"] = target.reshape(rows, columns).T
-        inputs[f"expand{t}"] = expand
-        inputs[f"project{t}"] = project
-        inputs[f"project_t{t}"] = project.T
+        loaded[f"expand{t}"] = expand
+        loaded[f"project{t}"] = project
+        loaded[f"target{t}"] = target.reshape(rows, columns)
+        scratch[f"expand_t{t}"] = pltpu.VMEM(expand.shape[::-1], BF16)
+        scratch[f"project_t{t}"] = pltpu.VMEM(project.shape[::-1], BF16)
+        scratch[f"target_t{t}"] = pltpu.VMEM((columns, rows), BF16)
         scratch[f"slope{t}"] = pltpu.VMEM((hidden, rows), F32)
         scratch[f"act{t}"] = pltpu.VMEM((hidden, rows), BF16)
         scratch[f"grad{t}"] = pltpu.VMEM((hidden, rows), BF16)
@@ -480,19 +515,23 @@
         scratch[f"from_x{t}"] = pltpu.VMEM((columns, rows), BF16)
         scratch[f"res{t}"] = pltpu.VMEM((features, rows), BF16)
         for i, size in ((2 * t, features // stores), (2 * t + 1, width // stores)):
-            outputs[f"out{i}"] = jax.ShapeDtypeStruct((size, hidden), F32)
+            shape = (hidden, size) if i % 2 == 0 else (size, hidden)
+            outputs[f"out{i}"] = jax.ShapeDtypeStruct(shape, F32)
             scratch[f"sum{i}"] = pltpu.VMEM((2, 2, 2, size, hidden), BF16)
             scratch[f"first{i}"] = pltpu.VMEM((2, 2, size, hidden), BF16)
             scratch[f"next{i}"] = pltpu.VMEM((2, size, hidden), BF16)
             scratch[f"last{i}"] = pltpu.VMEM((size, hidden), BF16)
-            orders.append((2, 1, 4) if i == 2 else (1, 2, 4))
-    names = list(inputs) + list(outputs) + list(scratch)
+            orders.append((2, 1, 4) if i in (0, 5) else (1, 2, 4))
+    for name, value in loaded.items():
+        scratch[name] = pltpu.VMEM(value.shape, BF16)
+    held = [name + "_hbm" for name in loaded]
+    names = list(inputs) + held + list(outputs) + list(scratch)
     vmem = pl.BlockSpec(memory_space=pltpu.VMEM)
     features = sum(project.shape[1] for project in projects)
     results = pl.pallas_call(
-        functools.partial(fused_kernel, names, orders),
+        functools.partial(fused_kernel, names, list(loaded), orders, capacity, patches),
         out_shape=tuple(outputs.values()),
-        in_specs=[vmem] * len(inputs),
+        in_specs=[vmem] * len(inputs) + [pl.BlockSpec(memory_space=pl.ANY)] * len(loaded),
         out_specs=tuple([vmem] * len(outputs)),
         scratch_shapes=list(scratch.values()),
         compiler_params=pltpu.CompilerParams(
@@ -503,16 +542,16 @@
             bytes_accessed=16 * 1024 * 1024,
             transcendentals=6 * rows * hidden,
         ),
-    )(*inputs.values())
+    )(*inputs.values(), *loaded.values())
     student_grad = results[0].reshape(student.shape[0], patches, quarter)
     return (
         student_grad,
+        results[6],
+        results[5],
+        results[4],
+        results[3],
         results[2],
-        results[1].T,
-        results[4],
-        results[3].T,
-        results[6],
-        results[5].T,
+        results[1],
     )
 
 

time: 195 us -> 154 us (0.79)
  Pallas kernels: 166 us -> 140 us
  local copies, waits for them, and re-layouts: 24.3 us -> 11.1 us
  other arithmetic: 2.51 us -> 0 us
    pallas_call x1, Pallas kernels: 166 us -> 140 us  [fused(): pl.pallas_call(functools.partial(fused_kernel, names, list(loaded), order...]
    reshape x3 -> x0, local copies, waits for them, and re-layouts: 5.58 us -> none  [fused(): inputs[f'target{t}'] = target.reshape(rows, columns).T]
    unnamed x22 -> x17, local copies, waits for them, and re-layouts: 14.3 us -> 10 us
where the time goes in v2:
time: 154 us; the launch traced here: 152 us
  Pallas kernels  140 us (91%)
  local copies, waits for them, and re-layouts  11.1 us (7%)
    pallas_call x1, Pallas kernels, fused(): pl.pallas_call(functools.partial(fused_kernel, names, list(loaded), order...  140 us
    unnamed x17, local copies, waits for them, and re-layouts  10 us

profile of v2, /device:TPU:0, one launch (start us, length us, event | category | flops | bytes accessed | tf_op | source)
XLA Modules:
  0.0 152.0 jit_solution(16680312455004059404)
XLA Ops:
  0.6 0.0 copy-start
  0.7 1.5 %copy-done = bf16[48,16,1280]{2,1,0:T(8,128)(2,1)S(1)} copy-done((bf16[48,16,1280]{2,1,0:T(8,128)(2,1)S(1)}, bf16[48,16,1280]{2,1,0:T(8,128)(2,1)}, u32[]{:S(2)}) %copy-start) | copy-done | bytes 1966104
  2.2 1.1 constant_dynamic-slice_fusion.refs_0_
  3.3 140.2 %shard_map.171 = (bf16[8,96,320]{2,1,0:T(8,128)(2,1)}, f32[384,128]{1,0:T(8,128)}, f32[160,384]{1,0:T(8,128)}, f32[384,144]{1,0:T(8,128)}, f32[160,384]{1,0:T(8,...) custom-call(bf16[8,96,320]{2,1,0:T(8,128)(2,1)} %constant_dynamic-slice_fusion.refs_0_, s32[1,256]{1,0:T(1,128)} %bitcast.12, ...), custom_call_target="tpu_custom_call" | custom-call | flops 8908701696 | bytes 16777216 | tf_op jit(solution)/shard_map/pallas_call | solution.py:531
  143.5 0.0 copy-start.3
  143.5 0.0 copy-start.2
  143.5 0.0 copy-start.1
  143.5 0.0 copy-start.4
  143.5 1.9 %copy.20 = f32[384,144]{0,1:T(8,128)} copy(f32[384,144]{1,0:T(8,128)} %get-tuple-element.25) | data formatting | bytes 442368
  145.4 1.9 %copy.19 = f32[384,192]{0,1:T(8,128)} copy(f32[384,192]{1,0:T(8,128)} %get-tuple-element.23) | data formatting | bytes 589824
  147.3 1.9 %copy.26 = bf16[48,16,320]{2,1,0:T(8,128)(2,1)} copy(bf16[48,16,320]{2,1,0:T(8,128)(2,1)} %bitcast.8) | data formatting | bytes 983040
  149.2 0.0 copy-done.3
  149.2 0.7 copy.27
  149.9 0.0 copy-done.2
  149.9 0.7 copy.28
  150.6 0.0 copy-done.1
  150.6 0.7 copy.29
  151.3 0.0 copy-done.4
  151.3 0.7 copy.30
Async XLA Ops:
  0.6 1.6 %copy-start = (bf16[48,16,1280]{2,1,0:T(8,128)(2,1)S(1)}, bf16[48,16,1280]{2,1,0:T(8,128)(2,1)}, u32[]{:S(2)}) copy-start(bf16[48,16,1280]{2,1,0:T(8,128)(2,1)} %param.12) | copy-start | bytes 5898244
  143.5 5.7 %copy-start.3 = (f32[160,384]{1,0:T(8,128)S(1)}, f32[160,384]{1,0:T(8,128)}, u32[]{:S(2)}) copy-start(f32[160,384]{1,0:T(8,128)} %get-tuple-element.36) | copy-start | bytes 737284
  143.5 6.4 %copy-start.2 = (f32[160,384]{1,0:T(8,128)S(1)}, f32[160,384]{1,0:T(8,128)}, u32[]{:S(2)}) copy-start(f32[160,384]{1,0:T(8,128)} %get-tuple-element.38) | copy-start | bytes 737284
  143.5 7.1 %copy-start.1 = (f32[160,384]{1,0:T(8,128)S(1)}, f32[160,384]{1,0:T(8,128)}, u32[]{:S(2)}) copy-start(f32[160,384]{1,0:T(8,128)} %get-tuple-element.40) | copy-start | bytes 737284
  143.5 7.8 %copy-start.4 = (f32[384,128]{1,0:T(8,128)S(1)}, f32[384,128]{1,0:T(8,128)}, u32[]{:S(2)}) copy-start(f32[384,128]{1,0:T(8,128)} %get-tuple-element.41) | copy-start | bytes 589828

commit v3 on v2

--- a/solution.py
+++ b/solution.py
@@ -238,12 +238,13 @@
     place = slot * patches + patch
     picked = lax.broadcasted_iota(jnp.int32, (slot_rows, row_total), 0) == place
     r["sel"][...] = picked.astype(F32).astype(BF16)
-    for name in names_loaded:
-        loads[name].wait()
-    for t in range(3):
-        r[f"expand_t{t}"][...] = r[f"expand{t}"][...].T
-        r[f"project_t{t}"][...] = r[f"project{t}"][...].T
-        r[f"target_t{t}"][...] = r[f"target{t}"][...].T
+
+    def turn(t):
+        for kind in ("expand", "project", "target"):
+            loads[f"{kind}{t}"].wait()
+            r[f"{kind}_t{t}"][...] = r[f"{kind}{t}"][...].T
+
+    turn(0)
     for copy in arrivals:
         copy.wait_recv()
     mine = rows_at(mp, quarter)
@@ -251,6 +252,7 @@
     xt[mine, :] = tn(xr[...].reshape(slot_rows, quarter), r["sel"][...]).astype(BF16)
     to_sibling = send(xt.at[mine, :], xt.at[mine, :], (dp, sibling))
     to_across = send(xt.at[mine, :], xt.at[mine, :], (dp, across))
+    turn(1)
     to_across.wait_recv()
     forward = send(xt.at[theirs, :], xt.at[theirs, :], (dp, sibling))
     to_sibling.wait_recv()
@@ -326,9 +328,7 @@
 
         def block(k, carry):
             a, b = k // 2, k % 2
-            total[own, a, b] = (
-                total[own, a, b].astype(F32) + landed[a, b].astype(F32)
-            ).astype(BF16)
+            total[own, a, b] = total[own, a, b] + landed[a, b]
             return carry
 
         lax.fori_loop(0, 4, block, 0)
@@ -342,9 +342,7 @@
         stage[i].wait_recv()
 
         def block(k, carry):
-            total[own, mid, k] = (
-                total[own, mid, k].astype(F32) + landed[k].astype(F32)
-            ).astype(BF16)
+            total[own, mid, k] = total[own, mid, k] + landed[k]
             return carry
 
         lax.fori_loop(0, 2, block, 0)
@@ -359,47 +357,62 @@
         summed = (
             total[own[0], own[1], own[2]].astype(F32) + r[f"last{i}"][...].astype(F32)
         ) * r["scale"][...]
-        r[f"out{i}"][...] = summed.T if i % 2 == 0 else summed
-
-    def grads(t):
-        res, act, grad = r[f"res{t}"], r[f"act{t}"], r[f"grad{t}"]
+        r[f"out{i}"][...] = summed.T if i == 0 else summed
+
+    def weight_grad(i, left, right):
+        total, order = r[f"sum{i}"], orders[i]
+        size = total.shape[3]
+
+        def block(k, carry):
+            both = nt(left[rows_at(k, 2 * size), :], right[...]).astype(BF16)
+            for low in (0, 1):
+                at = [bit_of(2 * k + low, bit) for bit in order]
+                total[at[0], at[1], at[2]] = both[low * size : (low + 1) * size]
+            return carry
+
+        lax.fori_loop(0, n_dp // 2, block, 0)
+
+    def project_grad(t):
         near, forwarded = gather[t]
         near.wait_recv()
         forwarded.wait_recv()
-        for i, left, right in ((2 * t, res, act), (2 * t + 1, xt, grad)):
-            total, order = r[f"sum{i}"], orders[i]
-            size = total.shape[3]
-            if right is grad:
-                back = nn(r[f"project{t}"][...], res[...])
-                grad[...] = (back * r[f"slope{t}"][...]).astype(BF16)
-
-            def block(k, carry):
-                both = nt(left[rows_at(k, 2 * size), :], right[...]).astype(BF16)
-                for low in (0, 1):
-                    at = [bit_of(2 * k + low, bit) for bit in order]
-                    total[at[0], at[1], at[2]] = both[low * size : (low + 1) * size]
-                return carry
-
-            lax.fori_loop(0, n_dp // 2, block, 0)
-            start_reduce(i)
+        weight_grad(2 * t, r[f"res{t}"], r[f"act{t}"])
+        start_reduce(2 * t)
+
+    def hidden_grad(t):
+        back = nn(r[f"project{t}"][...], r[f"res{t}"][...])
+        r[f"grad{t}"][...] = (back * r[f"slope{t}"][...]).astype(BF16)
+
+    def expand_grad(t):
+        weight_grad(2 * t + 1, xt, r[f"grad{t}"])
 
     first_half(0)
     to_x(0)
     first_half(1)
     residual(0)
-    to_x(1)
+    turn(2)
     first_half(2)
     pass_on(0)
+    to_x(1)
+    project_grad(0)
+    hidden_grad(0)
+    expand_grad(0)
+    start_reduce(1)
     residual(1)
+    second(0)
+    pass_on(1)
     to_x(2)
-    grads(0)
-    pass_on(1)
+    project_grad(1)
+    hidden_grad(1)
+    expand_grad(1)
+    second(1)
+    third(0)
     residual(2)
-    grads(1)
+    second(2)
+    start_reduce(3)
     pass_on(2)
-    second(0)
-    second(1)
-    grads(2)
+    project_grad(2)
+    hidden_grad(2)
 
     sp = r["sp"]
 
@@ -411,14 +424,14 @@
 
     lax.fori_loop(0, n_mp, block, 0)
     core_copy["s"] = send(sp.at[1 - core], r["sp_core"], (dp, sibling))
-    third(0)
-    second(2)
-    third(1)
+    expand_grad(2)
+    start_reduce(5)
     core_copy["s"].wait_recv()
     sp[core, 1 - x] = (
         sp[core, 1 - x].astype(F32) + r["sp_core"][1 - x].astype(F32)
     ).astype(BF16)
     x_copy["s"] = send(sp.at[core, 1 - x], r["sp_x"], (dp, across))
+    third(1)
     second(3)
     third(2)
     finish(0)
@@ -431,20 +444,31 @@
         send(r["home"].at[peer], r["student_out"].at[dp], (peer, mp)) for peer in dp_peers
     ]
     r["student_out"][dp] = r["home"][dp]
+    finish(1)
+    third(3)
+    second(5)
+    finish(2)
     second(4)
-    third(3)
-    finish(1)
-    second(5)
+    finish(3)
+    third(5)
     third(4)
-    finish(2)
-    third(5)
-    finish(3)
+    finish(5)
     finish(4)
-    finish(5)
     for copy in returns:
         copy.wait_recv()
     for copy in sent:
         copy.wait_send()
+
+
+def copy_kernel(*refs):
+    count = len(refs) // 2
+    copies = [
+        pltpu.make_async_copy(refs[i], refs[count + i], refs[-1].at[i]) for i in range(count)
+    ]
+    for copy in copies:
+        copy.start()
+    for copy in copies:
+        copy.wait()
 
 
 def fused(
@@ -515,7 +539,7 @@
         scratch[f"from_x{t}"] = pltpu.VMEM((columns, rows), BF16)
         scratch[f"res{t}"] = pltpu.VMEM((features, rows), BF16)
         for i, size in ((2 * t, features // stores), (2 * t + 1, width // stores)):
-            shape = (hidden, size) if i % 2 == 0 else (size, hidden)
+            shape = (hidden, size) if i == 0 else (size, hidden)
             outputs[f"out{i}"] = jax.ShapeDtypeStruct(shape, F32)
             scratch[f"sum{i}"] = pltpu.VMEM((2, 2, 2, size, hidden), BF16)
             scratch[f"first{i}"] = pltpu.VMEM((2, 2, size, hidden), BF16)
@@ -531,7 +555,7 @@
     results = pl.pallas_call(
         functools.partial(fused_kernel, names, list(loaded), orders, capacity, patches),
         out_shape=tuple(outputs.values()),
-        in_specs=[vmem] * len(inputs) + [pl.BlockSpec(memory_space=pl.ANY)] * len(loaded),
+        in_specs=[vmem] * len(inputs) + [pl.BlockSpec(memory_space=pltpu.HBM)] * len(loaded),
         out_specs=tuple([vmem] * len(outputs)),
         scratch_shapes=list(scratch.values()),
         compiler_params=pltpu.CompilerParams(
@@ -543,13 +567,22 @@
             transcendentals=6 * rows * hidden,
         ),
     )(*inputs.values(), *loaded.values())
+    anywhere = pl.BlockSpec(memory_space=pltpu.HBM)
+    results = pl.pallas_call(
+        copy_kernel,
+        out_shape=tuple(outputs.values()),
+        in_specs=[anywhere] * len(outputs),
+        out_specs=tuple([anywhere] * len(outputs)),
+        scratch_shapes=[pltpu.SemaphoreType.DMA((len(outputs),))],
+        compiler_params=pltpu.CompilerParams(vmem_limit_bytes=60 * 1024 * 1024),
+    )(*results)
     student_grad = results[0].reshape(student.shape[0], patches, quarter)
     return (
         student_grad,
         results[6],
-        results[5],
+        results[5].T,
         results[4],
-        results[3],
+        results[3].T,
         results[2],
         results[1],
     )

time: 154 us -> 208 us (1.35)
  Pallas kernels: 140 us -> 203 us
  local copies, waits for them, and re-layouts: 11.1 us -> 2.62 us
    pallas_call x0 -> x1, Pallas kernels: none -> 63 us  [fused(): pl.pallas_call(copy_kernel, out_shape=tuple(outputs.values()), in_specs=[...]
    unnamed x17 -> x2, local copies, waits for them, and re-layouts: 10 us -> 1.54 us
where the time goes in v3:
time: 208 us; the launch traced here: 206 us
  Pallas kernels  203 us (98%)
  local copies, waits for them, and re-layouts  2.62 us (1%)
    pallas_call x1, Pallas kernels, fused(): pl.pallas_call(functools.partial(fused_kernel, names, list(loaded), order...  140 us
    pallas_call x1, Pallas kernels, fused(): pl.pallas_call(copy_kernel, out_shape=tuple(outputs.values()), in_specs=[...  63 us

profile of v3, /device:TPU:0, one launch (start us, length us, event | category | flops | bytes accessed | tf_op | source)
XLA Modules:
  0.0 206.4 jit_solution(1187139101404856723)
XLA Ops:
  0.6 0.0 copy-start
  0.7 1.5 copy-done
  2.2 1.1 constant_dynamic-slice_fusion.refs_0_
  3.3 140.2 %shard_map.171 = (bf16[8,96,320]{2,1,0:T(8,128)(2,1)}, f32[384,128]{1,0:T(8,128)}, f32[160,384]{1,0:T(8,128)}, f32[144,384]{1,0:T(8,128)}, f32[160,384]{1,0:T(8,...) custom-call(bf16[8,96,320]{2,1,0:T(8,128)(2,1)} %constant_dynamic-slice_fusion.refs_0_, s32[1,256]{1,0:T(1,128)} %bitcast.16, ...), custom_call_target="tpu_custom_call" | custom-call | flops 8908701696 | bytes 16777216 | tf_op jit(solution)/shard_map/pallas_call | solution.py:555
  143.5 63.0 %shard_map.172 = (bf16[8,96,320]{2,1,0:T(8,128)(2,1)}, f32[384,128]{1,0:T(8,128)}, f32[160,384]{1,0:T(8,128)}, f32[144,384]{1,0:T(8,128)}, f32[160,384]{1,0:T(8,...) custom-call(bf16[8,96,320]{2,1,0:T(8,128)(2,1)} %get-tuple-element.21.refs_0_, f32[384,128]{1,0:T(8,128)} %get-tuple-element.22.refs_1_, ...), custom_call_target="tpu_custom_call" | custom-call | tf_op jit(solution)/shard_map/pallas_call | solution.py:571
Async XLA Ops:
  0.6 1.6 copy-start

commit v4 on v3

--- a/solution.py
+++ b/solution.py
@@ -245,6 +245,7 @@
             r[f"{kind}_t{t}"][...] = r[f"{kind}{t}"][...].T
 
     turn(0)
+    turn(1)
     for copy in arrivals:
         copy.wait_recv()
     mine = rows_at(mp, quarter)
@@ -252,7 +253,7 @@
     xt[mine, :] = tn(xr[...].reshape(slot_rows, quarter), r["sel"][...]).astype(BF16)
     to_sibling = send(xt.at[mine, :], xt.at[mine, :], (dp, sibling))
     to_across = send(xt.at[mine, :], xt.at[mine, :], (dp, across))
-    turn(1)
+    turn(2)
     to_across.wait_recv()
     forward = send(xt.at[theirs, :], xt.at[theirs, :], (dp, sibling))
     to_sibling.wait_recv()
@@ -390,26 +391,22 @@
     to_x(0)
     first_half(1)
     residual(0)
-    turn(2)
+    to_x(1)
     first_half(2)
     pass_on(0)
-    to_x(1)
     project_grad(0)
+    residual(1)
+    to_x(2)
     hidden_grad(0)
     expand_grad(0)
     start_reduce(1)
-    residual(1)
-    second(0)
     pass_on(1)
-    to_x(2)
     project_grad(1)
     hidden_grad(1)
+    residual(2)
     expand_grad(1)
-    second(1)
-    third(0)
-    residual(2)
-    second(2)
     start_reduce(3)
+    second(0)
     pass_on(2)
     project_grad(2)
     hidden_grad(2)
@@ -426,14 +423,15 @@
     core_copy["s"] = send(sp.at[1 - core], r["sp_core"], (dp, sibling))
     expand_grad(2)
     start_reduce(5)
+    second(1)
+    third(0)
     core_copy["s"].wait_recv()
     sp[core, 1 - x] = (
         sp[core, 1 - x].astype(F32) + r["sp_core"][1 - x].astype(F32)
     ).astype(BF16)
     x_copy["s"] = send(sp.at[core, 1 - x], r["sp_x"], (dp, across))
+    second(2)
     third(1)
-    second(3)
-    third(2)
     finish(0)
     own = sp[core, x].astype(F32) + r["sp_core"][x].astype(F32)
     x_copy["s"].wait_recv()
@@ -444,9 +442,11 @@
         send(r["home"].at[peer], r["student_out"].at[dp], (peer, mp)) for peer in dp_peers
     ]
     r["student_out"][dp] = r["home"][dp]
+    second(3)
+    third(2)
     finish(1)
+    second(5)
     third(3)
-    second(5)
     finish(2)
     second(4)
     finish(3)
@@ -461,13 +461,17 @@
 
 
 def copy_kernel(*refs):
-    count = len(refs) // 2
-    copies = [
-        pltpu.make_async_copy(refs[i], refs[count + i], refs[-1].at[i]) for i in range(count)
-    ]
-    for copy in copies:
+    count = len(refs) // 3
+    sources, results, held = refs[:count], refs[count : 2 * count], refs[2 * count : 3 * count]
+    entry, leave = refs[3 * count :]
+    arrive = [pltpu.make_async_copy(sources[i], held[i], entry.at[i]) for i in range(count)]
+    depart = [pltpu.make_async_copy(held[i], results[i], leave.at[i]) for i in range(count)]
+    for copy in arrive:
         copy.start()
-    for copy in copies:
+    for i in range(count):
+        arrive[i].wait()
+        depart[i].start()
+    for copy in depart:
         copy.wait()
 
 
@@ -573,7 +577,8 @@
         out_shape=tuple(outputs.values()),
         in_specs=[anywhere] * len(outputs),
         out_specs=tuple([anywhere] * len(outputs)),
-        scratch_shapes=[pltpu.SemaphoreType.DMA((len(outputs),))],
+        scratch_shapes=[pltpu.VMEM(value.shape, value.dtype) for value in outputs.values()]
+        + [pltpu.SemaphoreType.DMA((len(outputs),))] * 2,
         compiler_params=pltpu.CompilerParams(vmem_limit_bytes=60 * 1024 * 1024),
     )(*results)
     student_grad = results[0].reshape(student.shape[0], patches, quarter)

time: 208 us -> 156 us (0.75)
  Pallas kernels: 203 us -> 153 us
    pallas_call x1, Pallas kernels: 63 us -> 2.47 us  [fused(): pl.pallas_call(copy_kernel, out_shape=tuple(outputs.values()), in_specs=[...]
    pallas_call x1, Pallas kernels: 140 us -> 150 us  [fused(): pl.pallas_call(functools.partial(fused_kernel, names, list(loaded), order...]
where the time goes in v4:
time: 156 us
  Pallas kernels  153 us (98%)
  local copies, waits for them, and re-layouts  2.62 us (2%)
    pallas_call x1, Pallas kernels, fused(): pl.pallas_call(functools.partial(fused_kernel, names, list(loaded), order...  150 us

profile of v4, /device:TPU:0, one launch (start us, length us, event | category | flops | bytes accessed | tf_op | source)
XLA Modules:
  0.0 156.1 jit_solution(2580827309281520274)
XLA Ops:
  0.6 0.0 copy-start
  0.7 1.5 copy-done
  2.2 1.1 constant_dynamic-slice_fusion.refs_0_
  3.3 150.3 %shard_map.171 = (bf16[8,96,320]{2,1,0:T(8,128)(2,1)}, f32[384,128]{1,0:T(8,128)}, f32[160,384]{1,0:T(8,128)}, f32[144,384]{1,0:T(8,128)}, f32[160,384]{1,0:T(8,...) custom-call(bf16[8,96,320]{2,1,0:T(8,128)(2,1)} %constant_dynamic-slice_fusion.refs_0_, s32[1,256]{1,0:T(1,128)} %bitcast.16, ...), custom_call_target="tpu_custom_call" | custom-call | flops 8908701696 | bytes 16777216 | tf_op jit(solution)/shard_map/pallas_call | solution.py:559
  153.6 2.5 %shard_map.172 = (bf16[8,96,320]{2,1,0:T(8,128)(2,1)}, f32[384,128]{1,0:T(8,128)}, f32[160,384]{1,0:T(8,128)}, f32[144,384]{1,0:T(8,128)}, f32[160,384]{1,0:T(8,...) custom-call(bf16[8,96,320]{2,1,0:T(8,128)(2,1)} %get-tuple-element.21.refs_0_, f32[384,128]{1,0:T(8,128)} %get-tuple-element.22.refs_1_, ...), custom_call_target="tpu_custom_call" | custom-call | tf_op jit(solution)/shard_map/pallas_call | solution.py:575
Async XLA Ops:
  0.6 1.6 copy-start

commit v5 on v3

--- a/solution.py
+++ b/solution.py
@@ -461,13 +461,17 @@
 
 
 def copy_kernel(*refs):
-    count = len(refs) // 2
-    copies = [
-        pltpu.make_async_copy(refs[i], refs[count + i], refs[-1].at[i]) for i in range(count)
-    ]
-    for copy in copies:
+    count = len(refs) // 3
+    sources, results, held = refs[:count], refs[count : 2 * count], refs[2 * count : 3 * count]
+    entry, leave = refs[3 * count :]
+    arrive = [pltpu.make_async_copy(sources[i], held[i], entry.at[i]) for i in range(count)]
+    depart = [pltpu.make_async_copy(held[i], results[i], leave.at[i]) for i in range(count)]
+    for copy in arrive:
         copy.start()
-    for copy in copies:
+    for i in range(count):
+        arrive[i].wait()
+        depart[i].start()
+    for copy in depart:
         copy.wait()
 
 
@@ -573,7 +577,8 @@
         out_shape=tuple(outputs.values()),
         in_specs=[anywhere] * len(outputs),
         out_specs=tuple([anywhere] * len(outputs)),
-        scratch_shapes=[pltpu.SemaphoreType.DMA((len(outputs),))],
+        scratch_shapes=[pltpu.VMEM(value.shape, value.dtype) for value in outputs.values()]
+        + [pltpu.SemaphoreType.DMA((len(outputs),))] * 2,
         compiler_params=pltpu.CompilerParams(vmem_limit_bytes=60 * 1024 * 1024),
     )(*results)
     student_grad = results[0].reshape(student.shape[0], patches, quarter)

time: 208 us -> 147 us (0.71)
  Pallas kernels: 203 us -> 143 us
    pallas_call x1, Pallas kernels: 63 us -> 2.47 us  [fused(): pl.pallas_call(copy_kernel, out_shape=tuple(outputs.values()), in_specs=[...]
where the time goes in v5:
time: 147 us; the launch traced here: 146 us
  Pallas kernels  143 us (97%)
  local copies, waits for them, and re-layouts  2.62 us (2%)
    pallas_call x1, Pallas kernels, fused(): pl.pallas_call(functools.partial(fused_kernel, names, list(loaded), order...  140 us

profile of v5, /device:TPU:0, one launch (start us, length us, event | category | flops | bytes accessed | tf_op | source)
XLA Modules:
  0.0 145.9 jit_solution(4992761337167568186)
XLA Ops:
  0.6 0.0 copy-start
  0.7 1.5 %copy-done = bf16[48,16,1280]{2,1,0:T(8,128)(2,1)S(1)} copy-done((bf16[48,16,1280]{2,1,0:T(8,128)(2,1)S(1)}, bf16[48,16,1280]{2,1,0:T(8,128)(2,1)}, u32[]{:S(2)}) %copy-start) | copy-done | bytes 1966104
  2.2 1.1 constant_dynamic-slice_fusion.refs_0_
  3.3 140.2 %shard_map.171 = (bf16[8,96,320]{2,1,0:T(8,128)(2,1)}, f32[384,128]{1,0:T(8,128)}, f32[160,384]{1,0:T(8,128)}, f32[144,384]{1,0:T(8,128)}, f32[160,384]{1,0:T(8,...) custom-call(bf16[8,96,320]{2,1,0:T(8,128)(2,1)} %constant_dynamic-slice_fusion.refs_0_, s32[1,256]{1,0:T(1,128)} %bitcast.16, ...), custom_call_target="tpu_custom_call" | custom-call | flops 8908701696 | bytes 16777216 | tf_op jit(solution)/shard_map/pallas_call | solution.py:559
  143.5 2.5 %shard_map.172 = (bf16[8,96,320]{2,1,0:T(8,128)(2,1)}, f32[384,128]{1,0:T(8,128)}, f32[160,384]{1,0:T(8,128)}, f32[144,384]{1,0:T(8,128)}, f32[160,384]{1,0:T(8,...) custom-call(bf16[8,96,320]{2,1,0:T(8,128)(2,1)} %get-tuple-element.21.refs_0_, f32[384,128]{1,0:T(8,128)} %get-tuple-element.22.refs_1_, ...), custom_call_target="tpu_custom_call" | custom-call | tf_op jit(solution)/shard_map/pallas_call | solution.py:575
Async XLA Ops:
  0.6 1.6 %copy-start = (bf16[48,16,1280]{2,1,0:T(8,128)(2,1)S(1)}, bf16[48,16,1280]{2,1,0:T(8,128)(2,1)}, u32[]{:S(2)}) copy-start(bf16[48,16,1280]{2,1,0:T(8,128)(2,1)} %param.12) | copy-start | bytes 5898244
